TPU v7x, 32 devices: a whole 2x2x4 slice. The times are simulated.
32 devices in a mesh: dp: 8 (over z, x), ctx: 4 (over y, core).
Axes of the slice: x: 2, y: 2, z: 4, core: 2. Of those that a mesh axis runs over, the one named last changes fastest.
Arguments:
- rollout_rows: bfloat16 [8, 512, 5120], P('dp', 'ctx'), may hold values from -6 to 6
- dest_rank: int32 [8, 512], P('dp', 'ctx'), may hold values from 0 to 7, as said below
- doc_ids: int32 [8, 512], P('dp', 'ctx'), may hold values from 0 to 5, never falling along the last dimension, each value on 1 to 384 neighbouring positions
- advantage: float32 [8, 6], P('dp'), may hold values from -4 to 4
- out_grad: bfloat16 [8, 512, 4096], P('dp', 'ctx'), may hold values from -6 to 6
- q_gain: float32 [128], replicated, may hold values from 0.5 to 2
- k_gain: float32 [128], replicated, may hold values from 0.5 to 2
Outputs:
- attn_out: bfloat16 [8, 512, 4096], P('dp', 'ctx')
- packed_row_gradient: bfloat16 [8, 512, 5120], P('dp', 'ctx')
- q_gain_grad: float32 [128], replicated
- k_gain_grad: float32 [128], replicated
Inputs may be any that keep to these rules, and one draw needn't show every extreme that they name: `dest_rank`: at every position the 8 rows there go to 8 different ranks. From one device at most 16 rows go to any one other rank, and exactly 16 to one of them; any number of rows may stay. `doc_ids`: document numbers never fall along a pack; each document has at most 384 positions, one exactly 384.
All inputs are finite; a program needn't handle non-finite values.
Results may differ from a plain program's by a relative error of at most 0.014.
Values may be sent and summed in bfloat16 or wider, within the bound.
A program may use at most 64 MiB of HBM per device.

v0:
```python
import jax
import jax.numpy as jnp
from jax import lax
from jax.sharding import PartitionSpec as P

QUERY_HEADS = 32
KEY_VALUE_HEADS = 4
HEAD_SIZE = 128
DOCS = 6


epsilon = 1e-06


def passed_along(block, axis, distance):
    devices = range(lax.axis_size(axis))
    route = [(i - distance, i) for i in devices if i - distance in devices]
    return lax.ppermute(block, axis, route)


def rms_scale(values, scaling):
    return values * lax.rsqrt(jnp.mean(values * values, axis=-1, keepdims=True) + epsilon) * scaling


def per_device(rollout_rows, dest_rank, doc_ids, advantage, out_grad, q_gain, k_gain):
    n_ranks = lax.axis_size("dp")
    my_rank = lax.axis_index("dp")
    n_blocks = lax.axis_size("ctx")
    block_index = lax.axis_index("ctx")
    reach_blocks = min(4, n_blocks - 1)
    token_list = rollout_rows.shape[1]
    row_width = rollout_rows.shape[2]
    capacity = token_list // n_ranks
    query_groups = QUERY_HEADS // KEY_VALUE_HEADS
    inverse = HEAD_SIZE ** (-0.5)
    local_rows = rollout_rows[0]
    targets = dest_rank[0]
    one_hot = (targets[:, None] == jnp.arange(n_ranks, dtype=jnp.int32)[None, :]).astype(jnp.int32)
    places = jnp.sum((jnp.cumsum(one_hot, axis=0) - 1) * one_hot, axis=1)
    staying = targets == my_rank
    peer_index = jnp.where(staying, n_ranks, targets)
    slot_table = (
        jnp.full((n_ranks, capacity), -1, jnp.int32)
        .at[peer_index, places]
        .set(jnp.arange(token_list, dtype=jnp.int32), mode="drop")
    )
    outgoing = local_rows[jnp.maximum(slot_table, 0)]
    arrived, arrived_slots = (
        lax.all_to_all(outgoing, "dp", split_axis=0, concat_axis=0, tiled=True),
        lax.all_to_all(slot_table, "dp", split_axis=0, concat_axis=0, tiled=True),
    )
    flat_slots = arrived_slots.reshape(-1)
    packed_input = jnp.where(staying[:, None], local_rows, jnp.zeros_like(local_rows))
    packed_input = packed_input.at[jnp.where(flat_slots < 0, token_list, flat_slots)].set(
        arrived.reshape(-1, row_width), mode="drop"
    )
    q_raw = (
        packed_input[:, : QUERY_HEADS * HEAD_SIZE]
        .astype(jnp.float32)
        .reshape(token_list, QUERY_HEADS, HEAD_SIZE)
    )
    key_plain_rows = (
        packed_input[:, QUERY_HEADS * HEAD_SIZE : (QUERY_HEADS + KEY_VALUE_HEADS) * HEAD_SIZE]
        .astype(jnp.float32)
        .reshape(token_list, KEY_VALUE_HEADS, HEAD_SIZE)
    )
    value_row_block = packed_input[:, (QUERY_HEADS + KEY_VALUE_HEADS) * HEAD_SIZE :].reshape(
        token_list, KEY_VALUE_HEADS, HEAD_SIZE
    )
    q_normed, q_back = jax.vjp(rms_scale, q_raw, q_gain)
    k_normed, k_back = jax.vjp(rms_scale, key_plain_rows, k_gain)
    query_unit_rows = q_normed.astype(jnp.bfloat16)
    key_unit_rows = k_normed.astype(jnp.bfloat16)
    doc_tags = doc_ids[0] + 1
    pieces = [(key_unit_rows, value_row_block, doc_tags)]
    for distance in range(1, reach_blocks + 1):
        pieces.append(passed_along((key_unit_rows, value_row_block, doc_tags), "ctx", distance))
    key_rows = jnp.concatenate([piece[0] for piece in pieces], axis=0)
    value_rows = jnp.concatenate([piece[1] for piece in pieces], axis=0)
    key_tags = jnp.concatenate([piece[2] for piece in pieces], axis=0)
    q_pos = block_index * token_list + jnp.arange(token_list, dtype=jnp.int32)
    k_pos = jnp.concatenate([q_pos - distance * token_list for distance in range(reach_blocks + 1)])
    allowed = (doc_tags[:, None] == key_tags[None, :]) & (k_pos[None, :] <= q_pos[:, None])
    query_head_rows = jnp.moveaxis(
        query_unit_rows.reshape(token_list, KEY_VALUE_HEADS, query_groups, HEAD_SIZE), 1, 0
    )
    k_heads = jnp.moveaxis(key_rows, 1, 0)
    v_heads = jnp.moveaxis(value_rows, 1, 0)

    def head_forward(operands):
        q_part, k_part, v_part = operands
        scores = (
            jnp.einsum("tgd,sd->gts", q_part, k_part, preferred_element_type=jnp.float32) * inverse
        )
        weights = jnp.where(allowed[None], jnp.exp(scores), 0.0)
        numerator = jnp.einsum(
            "gts,sd->tgd", weights.astype(jnp.bfloat16), v_part, preferred_element_type=jnp.float32
        )
        return (numerator, jnp.sum(weights, axis=-1))

    numerator, totals = lax.map(head_forward, (query_head_rows, k_heads, v_heads))
    attention = (numerator / jnp.transpose(totals, (0, 2, 1))[..., None]).astype(jnp.bfloat16)
    attn_rows = jnp.moveaxis(attention, 0, 1).reshape(token_list, QUERY_HEADS * HEAD_SIZE)
    doc_hot = (doc_ids[0][:, None] == jnp.arange(DOCS, dtype=jnp.int32)[None, :]).astype(
        jnp.float32
    )
    adv_tok = jnp.sum(doc_hot * advantage[0][None, :], axis=1)
    output_gradient = (out_grad[0].astype(jnp.float32) * adv_tok[:, None]).astype(jnp.bfloat16)
    head_gradients = jnp.moveaxis(
        output_gradient.reshape(token_list, KEY_VALUE_HEADS, query_groups, HEAD_SIZE), 1, 0
    )
    deltas = jnp.sum(head_gradients.astype(jnp.float32) * attention.astype(jnp.float32), axis=-1)

    def head_backward(operands):
        q_part, k_part, v_part, d_part, delta_part, total_part = operands
        scores = (
            jnp.einsum("tgd,sd->gts", q_part, k_part, preferred_element_type=jnp.float32) * inverse
        )
        weights = jnp.where(allowed[None], jnp.exp(scores), 0.0)
        normalized = weights / total_part[:, :, None]
        dprobs = jnp.einsum("tgd,sd->gts", d_part, v_part, preferred_element_type=jnp.float32)
        dscores = (normalized * (dprobs - jnp.transpose(delta_part)[:, :, None])).astype(
            jnp.bfloat16
        )
        dq_part = (
            jnp.einsum("gts,sd->tgd", dscores, k_part, preferred_element_type=jnp.float32) * inverse
        )
        dk_part = (
            jnp.einsum("gts,tgd->sd", dscores, q_part, preferred_element_type=jnp.float32) * inverse
        )
        dv_part = jnp.einsum(
            "gts,tgd->sd",
            normalized.astype(jnp.bfloat16),
            d_part,
            preferred_element_type=jnp.float32,
        )
        return (dq_part, dk_part, dv_part)

    dq_heads, dk_heads, dv_heads = lax.map(
        head_backward, (query_head_rows, k_heads, v_heads, head_gradients, deltas, totals)
    )
    dq_hat = jnp.moveaxis(dq_heads, 0, 1).reshape(token_list, QUERY_HEADS, HEAD_SIZE)
    dk_blocks = jnp.moveaxis(dk_heads, 0, 1).astype(jnp.bfloat16)
    dv_blocks = jnp.moveaxis(dv_heads, 0, 1).astype(jnp.bfloat16)
    dk_total = lax.optimization_barrier(dk_blocks[:token_list]).astype(jnp.float32)
    value_gradient_total = lax.optimization_barrier(dv_blocks[:token_list]).astype(jnp.float32)
    for distance in range(1, reach_blocks + 1):
        returned = passed_along(
            (
                dk_blocks[distance * token_list : (distance + 1) * token_list],
                dv_blocks[distance * token_list : (distance + 1) * token_list],
            ),
            "ctx",
            -distance,
        )
        dk_total = dk_total + returned[0].astype(jnp.float32)
        value_gradient_total = value_gradient_total + returned[1].astype(jnp.float32)
    query_raw_gradient, q_gain_part = q_back(dq_hat)
    key_raw_gradient, k_gain_part = k_back(dk_total)
    q_gain_grad, k_gain_grad = lax.psum((q_gain_part, k_gain_part), ("dp", "ctx"))
    packed_row_gradient = jnp.concatenate(
        [
            query_raw_gradient.reshape(token_list, QUERY_HEADS * HEAD_SIZE),
            key_raw_gradient.reshape(token_list, KEY_VALUE_HEADS * HEAD_SIZE),
            value_gradient_total.reshape(token_list, KEY_VALUE_HEADS * HEAD_SIZE),
        ],
        axis=1,
    ).astype(jnp.bfloat16)
    return (attn_rows[None], packed_row_gradient[None], q_gain_grad, k_gain_grad)


def solution(mesh):
    placed = (
        P("dp", "ctx", None),
        P("dp", "ctx"),
        P("dp", "ctx"),
        P("dp", None),
        P("dp", "ctx", None),
        P(),
        P(),
    )
    return jax.shard_map(
        per_device,
        mesh=mesh,
        in_specs=placed,
        out_specs=(P("dp", "ctx", None), P("dp", "ctx", None), P(), P()),
        check_vma=False,
    )
```

profile of v0, /device:TPU:0, one launch (start us, length us, event | category | flops | bytes accessed | tf_op | source)
XLA Modules:
  0.0 245.2 jit_solution(12049442848570735904)
XLA Ops:
  1.4 2.3 collective-permute-start.3
  3.8 4.4 %collective-permute-start.4 = (s32[128]{0:T(128)S(1)}, s32[128]{0:T(128)S(1)}, u32[]{:S(2)}, u32[]{:S(2)}) collective-permute-start(s32[128]{0:T(128)S(1)} %broadcast_add_fusion.3), channel_id=1, source_target_pairs={{0,2},{1,3},{4,6},{5,7},{8,10},{9,11},{12,14},{13,15},{16,18},{17,... | collective-permute-start | bytes 1544 | tf_op jit(solution)/shard_map/ppermute | solution.py:18
  12.5 19.8 %scatter_fusion = s32[8,16]{1,0:T(8,128)} fusion(s32[8,16]{1,0:T(8,128)} %broadcast_in_dim.97, s32[128]{0:T(128)S(1)} %fusion.67, s32[128]{0:T(128)S(1)} %iota.16), kind=kCustom, calls=%fused_computation.1 | custom fusion | bytes 2560 | tf_op jit(solution)/shard_map/scatter | solution.py:45
  32.3 5.8 %all-to-all-start = ((s32[8,1,16]{2,1,0:T(1,128)}), s32[8,1,16]{2,1,0:T(1,128)S(1)}, u32[]{:S(2)}, u32[]{:S(2)}) async-start(s32[8,1,16]{2,1,0:T(1,128)} %bitcast.6), calls=%async_computation | async-start | bytes 8192 | tf_op jit(solution)/shard_map/all_to_all | solution.py:50
  39.0 2.4 gather_fusion
  41.4 3.2 %all-to-all-done = s32[8,1,16]{2,1,0:T(1,128)S(1)} async-done(((s32[8,1,16]{2,1,0:T(1,128)}), s32[8,1,16]{2,1,0:T(1,128)S(1)}, u32[]{:S(2)}, u32[]{:S(2)}) %all-to-all-start) | async-done | bytes 544 | tf_op jit(solution)/shard_map/all_to_all | solution.py:50
  44.5 4.3 %all-to-all-start.1 = ((bf16[8,16,5120]{2,1,0:T(8,128)(2,1)}), bf16[8,16,5120]{2,1,0:T(8,128)(2,1)}, u32[]{:S(2)}, u32[]{:S(2)}) async-start(bf16[8,16,5120]{2,1,0:T(8,128)(2,1)} %bitcast.8), calls=%async_computation.1 | async-start | bytes 2621440 | tf_op jit(solution)/shard_map/all_to_all | solution.py:49
  50.3 2.3 copy.172
  53.9 24.3 %all-to-all-done.1 = bf16[8,16,5120]{2,1,0:T(8,128)(2,1)} async-done(((bf16[8,16,5120]{2,1,0:T(8,128)(2,1)}), bf16[8,16,5120]{2,1,0:T(8,128)(2,1)}, u32[]{:S(2)}, u32[]{:S(2)}) %all-to-all-start.1) | async-done | bytes 1310752 | tf_op jit(solution)/shard_map/all_to_all | solution.py:49
  78.3 3.8 %scatter_fusion.1 = bf16[128,5120]{1,0:T(8,128)(2,1)S(1)} fusion(bf16[128,5120]{1,0:T(8,128)(2,1)S(1)} %broadcast_select_fusion, s32[128]{0:T(128)S(1)} %fusion.66, bf16[128,5120]{1,0:T(8,128)(2,1)} %bitcast.9), kind=kCustom, calls=%fused_computation.2 | custom fusion | bytes 3932672 | tf_op jit(solution)/shard_map/scatter | solution.py:54
  82.7 1.9 collective-permute-start.6
  84.6 2.2 collective-permute-start.7
  101.1 2.0 collective-permute-start.2
  103.1 2.0 fusion.54
  105.1 2.3 copy.171
  112.9 15.3 %while.28 = (s32[]{:T(128)}, f32[4,128,8,128]{1,3,2,0:T(8,128)S(1)}, f32[4,8,128]{2,1,0:T(8,128)}, bf16[4,512,128]{2,1,0:T(8,128)(2,1)}, bf16[4,512,128]{2,1,0:T...) while((s32[]{:T(128)}, ...), condition=%wide.region_8.9_spmd.clone, body=%wide.region_6.8_spmd.clone.sunk | while | flops 271776768 | bytes 5459565 | solution.py:101
  128.1 3.2 %multiply_reduce_fusion.1 = (f32[4,128,8]{1,2,0:T(8,128)S(1)}, bf16[4,128,8,128]{1,3,2,0:T(8,128)(2,1)}, bf16[4,128,8,128]{1,3,2,0:T(8,128)(2,1)}) fusion(f32[128]{0:T(128)S(1)} %copy-done.23, bf16[128,4,8,128]{0,3,2,1:T(8,128)(2,1)} %bitcast.249, f32[4,128,8,128]{1,3,2,0:T(8,128)S(1)} %get-tuple-element.101, f32[4,128,8]{1,2,0:T(8,128)} %bitcast.252), kind=kLoop, calls=%fused_computation.72 | loop fusion | flops 4714496 | bytes 5276160 | tf_op jit(solution)/shard_map/reduce_sum | solution.py:112
  131.6 34.6 %while.29 = (s32[]{:T(128)}, f32[4,128,8,128]{1,3,2,0:T(8,128)S(1)}, bf16[4,512,128]{2,1,0:T(8,128)(2,1)}, bf16[4,512,128]{2,1,0:T(8,128)(2,1)}, bf16[4,512,128]...) while((s32[]{:T(128)}, ...), condition=%wide.region_12.13_spmd.clone, body=%wide.region_11.12_spmd.clone.sunk | while | flops 675151872 | bytes 20482280 | solution.py:139
  172.1 2.4 fusion.53
  174.6 2.0 copy.177
  176.6 3.5 %multiply_reduce_fusion = f32[128,32]{1,0:T(8,128)} fusion(f32[128,32,128]{2,1,0:T(8,128)} %bitcast.245, f32[128,32,128]{2,1,0:T(8,128)} %copy.177, f32[128]{0:T(128)} %param.16), kind=kLoop, calls=%fused_computation.71 | loop fusion | flops 1568768 | bytes 4211200 | tf_op jit(solution)/shard_map/transpose(jvp())/reduce_sum | solution.py:22
  188.4 4.1 %fusion.56 = bf16[1,128,4096]{2,1,0:T(8,128)(2,1)S(1)} fusion(f32[16,8,32,128]{3,2,1,0:T(8,128)S(1)} %bitcast.247, f32[16,8,32,128]{3,2,1,0:T(8,128)S(1)} %bitcast.248, f32[128,4096]{1,0:T(8,128)S(1)} %copy-done.4, f32[4096]{0:T(1024)S(1)} %copy-done.13, bf16[128,5120]{1,0:T(8,128)(2,1)S(1)} %scatter_fusion.1), kind=kLoop, calls=%fused_computation.80 | loop fusion | flops 3670016 | bytes 8404992 | tf_op jit(solution)/shard_map/concatenate | solution.py:161
  201.9 3.7 %collective-permute-done.13 = bf16[128,4,128]{2,0,1:T(8,128)(2,1)S(1)} collective-permute-done((bf16[128,4,128]{2,0,1:T(8,128)(2,1)S(1)}, bf16[128,4,128]{2,0,1:T(8,128)(2,1)S(1)}, u32[]{:S(2)}, u32[]{:S(2)}) %collective-permute-start.13) | collective-permute-done | bytes 131104 | tf_op jit(solution)/shard_map/ppermute | solution.py:18
  207.0 37.0 %all-reduce = (f32[128]{0:T(128)}, f32[128]{0:T(128)}) all-reduce(f32[128]{0:T(128)S(1)} %copy-done.22, f32[128]{0:T(128)S(1)} %get-tuple-element.358), channel_id=1, replica_groups=mesh['dp'=8,'ctx'=4] {'dp','ctx'}, use_global_device_ids=true, to_apply=%region_16.17 | all-reduce | flops 256 | bytes 2048 | tf_op jit(solution)/shard_map/psum | solution.py:160
  (203 shorter events, 104.6 us)
Async XLA Ops:
  0.6 38.4 %copy-start = (bf16[1,128,5120]{2,1,0:T(8,128)(2,1)S(1)}, bf16[1,128,5120]{2,1,0:T(8,128)(2,1)}, u32[]{:S(2)}) copy-start(bf16[1,128,5120]{2,1,0:T(8,128)(2,1)} %param.11) | copy-start | bytes 3932164
  1.4 51.1 %collective-permute-start.3 = (s32[128]{0:T(128)S(1)}, s32[128]{0:T(128)S(1)}, u32[]{:S(2)}, u32[]{:S(2)}) collective-permute-start(s32[128]{0:T(128)S(1)} %broadcast_add_fusion.3), channel_id=1, source_target_pairs={{0,1},{1,2},{2,3},{4,5},{5,6},{6,7},{8,9},{9,10},{10,11},{12,13},{... | collective-permute-start | bytes 1544 | tf_op jit(solution)/shard_map/ppermute | solution.py:18
  3.8 48.8 %collective-permute-start.4 = (s32[128]{0:T(128)S(1)}, s32[128]{0:T(128)S(1)}, u32[]{:S(2)}, u32[]{:S(2)}) collective-permute-start(s32[128]{0:T(128)S(1)} %broadcast_add_fusion.3), channel_id=1, source_target_pairs={{0,2},{1,3},{4,6},{5,7},{8,10},{9,11},{12,14},{13,15},{16,18},{17,... | collective-permute-start | bytes 1544 | tf_op jit(solution)/shard_map/ppermute | solution.py:18
  8.2 44.3 %collective-permute-start.5 = (s32[128]{0:T(128)S(1)}, s32[128]{0:T(128)S(1)}, u32[]{:S(2)}, u32[]{:S(2)}) collective-permute-start(s32[128]{0:T(128)S(1)} %broadcast_add_fusion.3), channel_id=1, source_target_pairs={{0,3},{4,7},{8,11},{12,15},{16,19},{20,23},{24,27},{28,31}} | collective-permute-start | bytes 1544 | tf_op jit(solution)/shard_map/ppermute | solution.py:18
  32.3 12.2 %all-to-all-start = ((s32[8,1,16]{2,1,0:T(1,128)}), s32[8,1,16]{2,1,0:T(1,128)S(1)}, u32[]{:S(2)}, u32[]{:S(2)}) async-start(s32[8,1,16]{2,1,0:T(1,128)} %bitcast.6), calls=%async_computation | async-start | bytes 8192 | tf_op jit(solution)/shard_map/all_to_all | solution.py:50
  41.4 8.1 %copy-start.21 = (f32[128]{0:T(128)S(1)}, f32[128]{0:T(128)}, u32[]{:S(2)}) copy-start(f32[128]{0:T(128)} %param.16) | copy-start | bytes 1540
  44.5 33.7 %all-to-all-start.1 = ((bf16[8,16,5120]{2,1,0:T(8,128)(2,1)}), bf16[8,16,5120]{2,1,0:T(8,128)(2,1)}, u32[]{:S(2)}, u32[]{:S(2)}) async-start(bf16[8,16,5120]{2,1,0:T(8,128)(2,1)} %bitcast.8), calls=%async_computation.1 | async-start | bytes 2621440 | tf_op jit(solution)/shard_map/all_to_all | solution.py:49
  82.1 12.7 %copy-start.5 = (f32[16,4,8,128]{3,2,1,0:T(8,128)}, f32[16,4,8,128]{3,2,1,0:T(8,128)S(1)}, u32[]{:S(2)}) copy-start(f32[16,4,8,128]{3,2,1,0:T(8,128)S(1)} %get-tuple-element.418) | copy-start | bytes 786436
  82.5 12.4 %copy-start.16 = (f32[128,4]{0,1:T(4,128)}, f32[128,4]{0,1:T(4,128)S(1)}, u32[]{:S(2)}) copy-start(f32[128,4]{0,1:T(4,128)S(1)} %copy.166) | copy-start | bytes 6148
  82.5 12.3 %copy-start.14 = (f32[128,4]{0,1:T(4,128)}, f32[128,4]{0,1:T(4,128)S(1)}, u32[]{:S(2)}) copy-start(f32[128,4]{0,1:T(4,128)S(1)} %fusion.64) | copy-start | bytes 6148
  82.7 18.5 %collective-permute-start.6 = (bf16[128,4,128]{2,0,1:T(8,128)(2,1)S(1)}, bf16[128,4,128]{2,0,1:T(8,128)(2,1)}, u32[]{:S(2)}, u32[]{:S(2)}) collective-permute-start(bf16[128,4,128]{2,0,1:T(8,128)(2,1)S(1)} %multiply_convert_fusion.1), channel_id=1, source_target_pairs={{0,1},{1,2},{2,3},{4,5},{5,6},{6,7},{8,9},{9,10},{10,11},{12,13},{... | collective-permute-start | bytes 393224 | tf_op jit(solution)/shard_map/ppermute | solution.py:18
  84.6 24.2 %collective-permute-start.7 = (bf16[128,4,128]{2,0,1:T(8,128)(2,1)S(1)}, bf16[128,4,128]{2,0,1:T(8,128)(2,1)}, u32[]{:S(2)}, u32[]{:S(2)}) collective-permute-start(bf16[128,4,128]{2,0,1:T(8,128)(2,1)S(1)} %multiply_convert_fusion.1), channel_id=1, source_target_pairs={{0,2},{1,3},{4,6},{5,7},{8,10},{9,11},{12,14},{13,15},{16,18},{17,... | collective-permute-start | bytes 393224 | tf_op jit(solution)/shard_map/ppermute | solution.py:18
  86.8 22.0 %collective-permute-start.8 = (bf16[128,4,128]{2,0,1:T(8,128)(2,1)S(1)}, bf16[128,4,128]{2,0,1:T(8,128)(2,1)}, u32[]{:S(2)}, u32[]{:S(2)}) collective-permute-start(bf16[128,4,128]{2,0,1:T(8,128)(2,1)S(1)} %multiply_convert_fusion.1), channel_id=1, source_target_pairs={{0,3},{4,7},{8,11},{12,15},{16,19},{20,23},{24,27},{28,31}} | collective-permute-start | bytes 393224 | tf_op jit(solution)/shard_map/ppermute | solution.py:18
  89.4 21.3 %collective-permute-start = (bf16[128,4,128]{2,0,1:T(8,128)(2,1)}, bf16[128,4,128]{2,0,1:T(8,128)(2,1)}, u32[]{:S(2)}, u32[]{:S(2)}) collective-permute-start(bf16[128,4,128]{2,0,1:T(8,128)(2,1)} %bitcast.192), channel_id=1, source_target_pairs={{0,1},{1,2},{2,3},{4,5},{5,6},{6,7},{8,9},{9,10},{10,11},{12,13},{... | collective-permute-start | bytes 393224 | tf_op jit(solution)/shard_map/ppermute | solution.py:18
  91.3 19.4 %collective-permute-start.1 = (bf16[128,4,128]{2,0,1:T(8,128)(2,1)}, bf16[128,4,128]{2,0,1:T(8,128)(2,1)}, u32[]{:S(2)}, u32[]{:S(2)}) collective-permute-start(bf16[128,4,128]{2,0,1:T(8,128)(2,1)} %bitcast.192), channel_id=1, source_target_pairs={{0,2},{1,3},{4,6},{5,7},{8,10},{9,11},{12,14},{13,15},{16,18},{17,... | collective-permute-start | bytes 393224 | tf_op jit(solution)/shard_map/ppermute | solution.py:18
  101.1 9.6 %collective-permute-start.2 = (bf16[128,4,128]{2,0,1:T(8,128)(2,1)}, bf16[128,4,128]{2,0,1:T(8,128)(2,1)}, u32[]{:S(2)}, u32[]{:S(2)}) collective-permute-start(bf16[128,4,128]{2,0,1:T(8,128)(2,1)} %bitcast.192), channel_id=1, source_target_pairs={{0,3},{4,7},{8,11},{12,15},{16,19},{20,23},{24,27},{28,31}} | collective-permute-start | bytes 393224 | tf_op jit(solution)/shard_map/ppermute | solution.py:18
  112.9 15.3 %copy-start.23 = (f32[128]{0:T(128)S(1)}, f32[128]{0:T(128)}, u32[]{:S(2)}) copy-start(f32[128]{0:T(128)} %select_reduce_fusion.1) | copy-start | bytes 1540
  168.0 29.7 %collective-permute-start.10 = (bf16[128,4,128]{2,0,1:T(8,128)(2,1)}, bf16[128,4,128]{2,0,1:T(8,128)(2,1)}, u32[]{:S(2)}, u32[]{:S(2)}) collective-permute-start(bf16[128,4,128]{2,0,1:T(8,128)(2,1)} %get-tuple-element.422), channel_id=1, source_target_pairs={{2,0},{3,1},{6,4},{7,5},{10,8},{11,9},{14,12},{15,13},{18,16},{19,... | collective-permute-start | bytes 393224 | tf_op jit(solution)/shard_map/ppermute | solution.py:18
  169.3 29.8 %collective-permute-start.11 = (bf16[128,4,128]{2,0,1:T(8,128)(2,1)}, bf16[128,4,128]{2,0,1:T(8,128)(2,1)}, u32[]{:S(2)}, u32[]{:S(2)}) collective-permute-start(bf16[128,4,128]{2,0,1:T(8,128)(2,1)} %get-tuple-element.421), channel_id=1, source_target_pairs={{3,0},{7,4},{11,8},{15,12},{19,16},{23,20},{27,24},{31,28}} | collective-permute-start | bytes 393224 | tf_op jit(solution)/shard_map/ppermute | solution.py:18
  170.6 28.5 %collective-permute-start.9 = (bf16[128,4,128]{2,0,1:T(8,128)(2,1)}, bf16[128,4,128]{2,0,1:T(8,128)(2,1)}, u32[]{:S(2)}, u32[]{:S(2)}) collective-permute-start(bf16[128,4,128]{2,0,1:T(8,128)(2,1)} %get-tuple-element.423), channel_id=1, source_target_pairs={{1,0},{2,1},{3,2},{5,4},{6,5},{7,6},{9,8},{10,9},{11,10},{13,12},{... | collective-permute-start | bytes 393224 | tf_op jit(solution)/shard_map/ppermute | solution.py:18
  193.8 8.1 %collective-permute-start.12 = (bf16[128,4,128]{2,0,1:T(8,128)(2,1)S(1)}, bf16[128,4,128]{2,0,1:T(8,128)(2,1)S(1)}, u32[]{:S(2)}, u32[]{:S(2)}) collective-permute-start(bf16[128,4,128]{2,0,1:T(8,128)(2,1)S(1)} %get-tuple-element.427), channel_id=1, source_target_pairs={{1,0},{2,1},{3,2},{5,4},{6,5},{7,6},{9,8},{10,9},{11,10},{13,12},{... | collective-permute-start | bytes 393224 | tf_op jit(solution)/shard_map/ppermute | solution.py:18
  195.1 10.5 %collective-permute-start.13 = (bf16[128,4,128]{2,0,1:T(8,128)(2,1)S(1)}, bf16[128,4,128]{2,0,1:T(8,128)(2,1)S(1)}, u32[]{:S(2)}, u32[]{:S(2)}) collective-permute-start(bf16[128,4,128]{2,0,1:T(8,128)(2,1)S(1)} %get-tuple-element.426), channel_id=1, source_target_pairs={{2,0},{3,1},{6,4},{7,5},{10,8},{11,9},{14,12},{15,13},{18,16},{19,... | collective-permute-start | bytes 393224 | tf_op jit(solution)/shard_map/ppermute | solution.py:18
  197.7 9.3 %copy-start.22 = (f32[128]{0:T(128)S(1)}, f32[128]{0:T(128)}, u32[]{:S(2)}) copy-start(f32[128]{0:T(128)} %fusion.53) | copy-start | bytes 1540
  197.7 9.0 %collective-permute-start.14 = (bf16[128,4,128]{2,0,1:T(8,128)(2,1)S(1)}, bf16[128,4,128]{2,0,1:T(8,128)(2,1)S(1)}, u32[]{:S(2)}, u32[]{:S(2)}) collective-permute-start(bf16[128,4,128]{2,0,1:T(8,128)(2,1)S(1)} %get-tuple-element.425), channel_id=1, source_target_pairs={{3,0},{7,4},{11,8},{15,12},{19,16},{23,20},{27,24},{31,28}} | collective-permute-start | bytes 393224 | tf_op jit(solution)/shard_map/ppermute | solution.py:18
  (28 other events, 105.6 us)
where the time goes:
time: 248 us; the launch traced here: 245 us
  local copies, waits for them, and re-layouts  61.7 us (25%)
  matrix products  39.3 us (16%)
  starting transfers between devices  38.1 us (15%)
  blocking collectives  37 us (15%)
  other arithmetic  35.1 us (14%)
  waiting for transfers between devices  32.4 us (13%)
    psum x1, blocking collectives, per_device(): lax.psum((q_gain_part, k_gain_part), ('dp', 'ctx'))  37 us
    ppermute x15, starting transfers between devices, passed_along(): return lax.ppermute(block, axis, route)  28 us
    all_to_all x1, waiting for transfers between devices, per_device(): lax.all_to_all(outgoing, 'dp', split_axis=0, concat_axis=0, tiled=True)  24.3 us
    scatter x1, local copies, waits for them, and re-layouts, per_device(): slot_table = jnp.full((n_ranks, capacity), -1, jnp.int32).at[peer_index,...  19.8 us
    unnamed x50, local copies, waits for them, and re-layouts  7.64 us
    reduce_sum x3, other arithmetic, rms_scale(): values * lax.rsqrt(jnp.mean(values * values, axis=-1, keepdims=True) + ep...  7.17 us
    dot_general x4, matrix products, head_backward(): jnp.einsum('tgd,sd->gts', q_part, k_part, preferred_element_type=jnp.floa...  6.66 us
    dot_general x4, matrix products, head_forward(): jnp.einsum('tgd,sd->gts', q_part, k_part, preferred_element_type=jnp.floa...  6.35 us
  transfers between devices with their start and end apart: 17, of which 4 were waited for; matrix products, arithmetic and copies ran while one was open for 29% of the time, Pallas kernels for 0%

commit v1 on v0

v1 whole, which is shorter than its diff:
```python
import functools
import math

import jax
import jax.numpy as jnp
from jax import lax
from jax.experimental import pallas as pl
from jax.experimental.pallas import tpu as pltpu
from jax.sharding import PartitionSpec as P

QUERY_HEADS = 32
KEY_VALUE_HEADS = 4
HEAD_SIZE = 128
GROUP = QUERY_HEADS // KEY_VALUE_HEADS
GROUP_WIDTH = GROUP * HEAD_SIZE
QUERY_WIDTH = QUERY_HEADS * HEAD_SIZE
KEY_WIDTH = KEY_VALUE_HEADS * HEAD_SIZE
CHUNKS = KEY_VALUE_HEADS + 1

epsilon = 1e-06
f32 = jnp.float32
bf16 = jnp.bfloat16
MESH = pl.DeviceIdType.MESH
LAST = (((1,), (1,)), ((), ()))


def matmul(a, b):
    return jnp.dot(a, b, preferred_element_type=f32)


def matmul_last(a, b):
    return lax.dot_general(a, b, LAST, preferred_element_type=f32)


def kernel(
    n_ranks, n_blocks, reach, capacity, pitch,
    rows_ref, dest_ref, docs_ref, adv_ref, grad_ref, q_gain_ref, k_gain_ref,
    attn_ref, out_ref, q_sum_ref, k_sum_ref,
    dest_all, docs_all, send, recv, place, kv_raw, kv_win, allowed,
    prob_s, dscore_s, q_s, d_s, part, ret, gain_ctx, gain_dp,
    dest_send, dest_recv, docs_send, docs_recv, row_send, row_recv,
    kv_send, kv_recv, ret_send, ret_recv, gc_send, gc_recv, gd_send, gd_recv,
):
    tokens = rows_ref.shape[1]
    keys = (reach + 1) * tokens
    me = lax.axis_index("dp")
    block = lax.axis_index("ctx")
    inverse = HEAD_SIZE ** (-0.5)

    barrier = pltpu.get_barrier_semaphore()

    def greet_dp(o, _):
        pl.semaphore_signal(
            barrier, inc=1, device_id={"dp": lax.rem(me + o, n_ranks)}, device_id_type=MESH
        )
        return 0

    def greet_ctx(o, _):
        pl.semaphore_signal(
            barrier, inc=1, device_id={"ctx": lax.rem(block + o, n_blocks)}, device_id_type=MESH
        )
        return 0

    lax.fori_loop(1, n_ranks, greet_dp, 0)
    lax.fori_loop(1, n_blocks, greet_ctx, 0)

    dest_all[me] = dest_ref[...]
    docs_all[0] = docs_ref[...]
    gain_ctx[block] = jnp.zeros((8, HEAD_SIZE), f32)
    for c in range(CHUNKS):
        recv[c, pl.ds(pl.multiple_of(me * pitch, 16), pitch), :] = jnp.zeros(
            (pitch, GROUP_WIDTH), bf16
        )
    for d in range(1, reach + 1):

        @pl.when(block < d)
        def _():
            docs_all[d] = jnp.full((1, tokens), -1, jnp.int32)
            kv_win[:, d * tokens : (d + 1) * tokens, :] = jnp.zeros(
                (KEY_VALUE_HEADS, tokens, 2 * HEAD_SIZE), bf16
            )

        @pl.when(block + d >= n_blocks)
        def _():
            ret[d - 1] = jnp.zeros((KEY_VALUE_HEADS, tokens, 2 * HEAD_SIZE), bf16)

    slots = n_ranks * pitch
    slot_row = lax.broadcasted_iota(jnp.int32, (slots, tokens), 0)
    slot_rank = slot_row // pitch
    slot_place = (slot_row % pitch).astype(f32)
    earlier = (
        lax.broadcasted_iota(jnp.int32, (tokens, tokens), 0)
        <= lax.broadcasted_iota(jnp.int32, (tokens, tokens), 1)
    ).astype(f32).astype(bf16)
    diagonal = lax.broadcasted_iota(jnp.int32, (tokens, tokens), 0) == lax.broadcasted_iota(
        jnp.int32, (tokens, tokens), 1
    )

    def slot_table(hit):
        hits = jnp.where(hit, 1.0, 0.0)
        count = matmul(hits.astype(bf16), earlier)
        return jnp.where(count - 1.0 == slot_place, hits, 0.0)

    def column(row):
        return jnp.sum(jnp.where(diagonal, row.astype(f32), 0.0), axis=1, keepdims=True)

    going = slot_table((dest_ref[...] == slot_rank) & (slot_rank != me)).astype(bf16)

    pl.semaphore_wait(barrier, n_ranks - 1 + n_blocks - 1)

    def dest_copy(src, dst, to):
        return pltpu.make_async_remote_copy(
            src_ref=dest_all.at[src],
            dst_ref=dest_all.at[src],
            send_sem=dest_send.at[dst],
            recv_sem=dest_recv.at[src],
            device_id={"dp": to},
            device_id_type=MESH,
        )

    def row_copy(c, slot, home, to):
        return pltpu.make_async_remote_copy(
            src_ref=send.at[c, pl.ds(pl.multiple_of(slot * pitch, 16), pitch), :],
            dst_ref=recv.at[c, pl.ds(pl.multiple_of(home * pitch, 16), pitch), :],
            send_sem=row_send.at[c, slot],
            recv_sem=row_recv.at[c, home],
            device_id={"dp": to},
            device_id_type=MESH,
        )

    def docs_copy(d, to):
        return pltpu.make_async_remote_copy(
            src_ref=docs_all.at[0],
            dst_ref=docs_all.at[d],
            send_sem=docs_send.at[d - 1],
            recv_sem=docs_recv.at[d - 1],
            device_id={"ctx": to},
            device_id_type=MESH,
        )

    def kv_copy(d, to):
        return pltpu.make_async_remote_copy(
            src_ref=kv_win.at[:, pl.ds(0, tokens), :],
            dst_ref=kv_win.at[:, pl.ds(d * tokens, tokens), :],
            send_sem=kv_send.at[d - 1],
            recv_sem=kv_recv.at[d - 1],
            device_id={"ctx": to},
            device_id_type=MESH,
        )

    def ret_copy(d, g, to):
        return pltpu.make_async_remote_copy(
            src_ref=part.at[g, pl.ds(d * tokens, tokens), :],
            dst_ref=ret.at[d - 1, g],
            send_sem=ret_send.at[d - 1, g],
            recv_sem=ret_recv.at[d - 1, g],
            device_id={"ctx": to},
            device_id_type=MESH,
        )

    def loop(stop, body):
        def step(o, _):
            body(o)
            return 0

        lax.fori_loop(1, stop, step, 0)

    def ahead(o):
        return lax.rem(me + o, n_ranks)

    loop(n_ranks, lambda o: dest_copy(me, ahead(o), ahead(o)).start())
    for d in range(1, reach + 1):

        @pl.when(block + d < n_blocks)
        def _():
            docs_copy(d, block + d).start()

    for c in range(CHUNKS):
        first = QUERY_WIDTH if c == 0 else (c - 1) * GROUP_WIDTH
        send[c] = matmul(going, rows_ref[0, :, first : first + GROUP_WIDTH]).astype(bf16)
        loop(n_ranks, lambda o: row_copy(c, ahead(o), me, ahead(o)).start())

    loop(n_ranks, lambda o: dest_copy(ahead(o), me, ahead(o)).wait_recv())
    source = jnp.broadcast_to(dest_all[...], (n_ranks, pitch, tokens)).reshape(slots, tokens)
    coming = slot_table((source == me) & (slot_rank != me))
    place[...] = jnp.transpose(coming).astype(bf16)
    staying = column(jnp.where(dest_ref[...] == me, 1.0, 0.0))
    doc_column = column(docs_ref[...])
    advantage = jnp.zeros((tokens, 1), f32)
    for doc in range(adv_ref.shape[1]):
        advantage = advantage + jnp.where(
            doc_column == float(doc), adv_ref[0:1, doc : doc + 1], 0.0
        )

    def packed(c, first):
        loop(n_ranks, lambda o: row_copy(c, me, ahead(o), ahead(o)).wait_recv())
        local = rows_ref[0, :, pl.ds(first, GROUP_WIDTH)].astype(f32)
        return matmul(place[...], recv[c]) + local * staying

    def unit(values):
        scale = lax.rsqrt(jnp.mean(values * values, axis=-1, keepdims=True) + epsilon)
        return values * scale, scale

    kv = packed(0, QUERY_WIDTH)
    kv_raw[...] = kv
    for g in range(KEY_VALUE_HEADS):
        k_unit, _ = unit(kv[:, g * HEAD_SIZE : (g + 1) * HEAD_SIZE])
        kv_win[g, 0:tokens, 0:HEAD_SIZE] = (k_unit * k_gain_ref[...]).astype(bf16)
        kv_win[g, 0:tokens, HEAD_SIZE : 2 * HEAD_SIZE] = kv[
            :, KEY_WIDTH + g * HEAD_SIZE : KEY_WIDTH + (g + 1) * HEAD_SIZE
        ].astype(bf16)
    for d in range(1, reach + 1):

        @pl.when(block + d < n_blocks)
        def _():
            kv_copy(d, block + d).start()

    for d in range(1, reach + 1):

        @pl.when(block >= d)
        def _():
            docs_copy(d, block - d).wait_recv()

    my_docs = docs_ref[...].astype(f32)
    for d in range(reach + 1):
        same = column(docs_all[d]) == my_docs
        if d == 0:
            same = same & (
                lax.broadcasted_iota(jnp.int32, (tokens, tokens), 0)
                <= lax.broadcasted_iota(jnp.int32, (tokens, tokens), 1)
            )
        same = jnp.where(same, 1.0, 0.0)
        allowed[d * tokens : (d + 1) * tokens, 0:tokens] = same
        allowed[d * tokens : (d + 1) * tokens, tokens : 2 * tokens] = same

    for d in range(1, reach + 1):

        @pl.when(block >= d)
        def _():
            kv_copy(d, block - d).wait_recv()

    def one_group(g, q_gain_sum):
        first = pl.multiple_of(g * GROUP_WIDTH, GROUP_WIDTH)
        raw = packed(g + 1, first)
        grads = (
            grad_ref[0, :, pl.ds(first, GROUP_WIDTH)].astype(f32) * advantage
        ).astype(bf16)
        k = kv_win[g, :, 0:HEAD_SIZE]
        v = kv_win[g, :, HEAD_SIZE : 2 * HEAD_SIZE]
        k_across = jnp.transpose(k.astype(f32)).astype(bf16)
        v_across = jnp.transpose(v.astype(f32)).astype(bf16)
        for pair in range(GROUP // 2):
            a = slice(2 * pair * HEAD_SIZE, (2 * pair + 1) * HEAD_SIZE)
            b = slice((2 * pair + 1) * HEAD_SIZE, (2 * pair + 2) * HEAD_SIZE)
            across = slice(pair * 2 * tokens, (pair + 1) * 2 * tokens)
            q_unit, q_scale = unit(jnp.concatenate([raw[:, a], raw[:, b]], axis=0))
            q_hat = (q_unit * q_gain_ref[...]).astype(bf16)
            d_out = jnp.concatenate([grads[:, a], grads[:, b]], axis=0)
            score = matmul_last(k, q_hat)
            weight = jnp.exp2(score * (inverse * math.log2(math.e))) * allowed[...]
            total = jnp.sum(weight, axis=0, keepdims=True)
            share = 1.0 / total
            attn = (matmul(v_across, weight.astype(bf16)) * share).astype(bf16).astype(f32)
            delta = jnp.sum(jnp.transpose(d_out.astype(f32)) * attn, axis=0, keepdims=True)
            attn_rows = jnp.transpose(attn).astype(bf16)
            prob = weight * share
            dscore = (prob * (matmul_last(v, d_out) - delta)).astype(bf16)
            prob_s[:, across] = prob.astype(bf16)
            dscore_s[:, across] = dscore
            q_s[across, :] = q_hat
            d_s[across, :] = d_out
            dq_hat = jnp.transpose(matmul(k_across, dscore)) * inverse
            q_gain_sum = q_gain_sum + jnp.sum(dq_hat * q_unit, axis=0, keepdims=True)
            scaled = dq_hat * q_gain_ref[...]
            dq = (
                q_scale * (scaled - q_unit * jnp.mean(scaled * q_unit, axis=-1, keepdims=True))
            ).astype(bf16)
            for half, where in ((0, a), (1, b)):
                cols = pl.ds(pl.multiple_of(first + where.start, HEAD_SIZE), HEAD_SIZE)
                attn_ref[0, :, cols] = attn_rows[half * tokens : (half + 1) * tokens]
                out_ref[0, :, cols] = dq[half * tokens : (half + 1) * tokens]
        part[g, :, 0:HEAD_SIZE] = (matmul(dscore_s[...], q_s[...]) * inverse).astype(bf16)
        part[g, :, HEAD_SIZE : 2 * HEAD_SIZE] = matmul(prob_s[...], d_s[...]).astype(bf16)
        for d in range(1, reach + 1):

            @pl.when(block >= d)
            def _():
                ret_copy(d, g, block - d).start()

        return q_gain_sum

    q_gain_sum = lax.fori_loop(0, KEY_VALUE_HEADS, one_group, jnp.zeros((1, HEAD_SIZE), f32))

    for d in range(1, reach + 1):

        @pl.when(block + d < n_blocks)
        def _():
            for g in range(KEY_VALUE_HEADS):
                ret_copy(d, g, block + d).wait_recv()

    k_gain_sum = jnp.zeros((1, HEAD_SIZE), f32)
    for g in range(KEY_VALUE_HEADS):
        both = part[g, 0:tokens, :].astype(f32)
        for d in range(1, reach + 1):
            both = both + ret[d - 1, g].astype(f32)
        dk_hat = both[:, 0:HEAD_SIZE]
        k_unit, k_scale = unit(kv_raw[:, g * HEAD_SIZE : (g + 1) * HEAD_SIZE])
        k_gain_sum = k_gain_sum + jnp.sum(dk_hat * k_unit, axis=0, keepdims=True)
        scaled = dk_hat * k_gain_ref[...]
        dk = k_scale * (scaled - k_unit * jnp.mean(scaled * k_unit, axis=-1, keepdims=True))
        at = QUERY_WIDTH + g * HEAD_SIZE
        out_ref[0, :, at : at + HEAD_SIZE] = dk.astype(bf16)
        at = at + KEY_WIDTH
        out_ref[0, :, at : at + HEAD_SIZE] = both[:, HEAD_SIZE:].astype(bf16)

    def gain_copy(buffer, send_sems, recv_sems, axis, home, to):
        return pltpu.make_async_remote_copy(
            src_ref=buffer.at[home],
            dst_ref=buffer.at[home],
            send_sem=send_sems.at[to],
            recv_sem=recv_sems.at[home],
            device_id={axis: to},
            device_id_type=MESH,
        )

    def exchange(buffer, send_sems, recv_sems, axis, mine, count):
        def other(o):
            return lax.rem(mine + o, count)

        loop(count, lambda o: gain_copy(buffer, send_sems, recv_sems, axis, mine, other(o)).start())

        def arrive(o):
            pltpu.make_async_remote_copy(
                src_ref=buffer.at[mine],
                dst_ref=buffer.at[other(o)],
                send_sem=send_sems.at[other(o)],
                recv_sem=recv_sems.at[other(o)],
                device_id={axis: other(o)},
                device_id_type=MESH,
            ).wait_recv()

        loop(count, arrive)
        total = buffer[0]
        for i in range(1, count):
            total = total + buffer[i]
        return total

    gain_ctx[block, 0:1, :] = q_gain_sum
    gain_ctx[block, 1:2, :] = k_gain_sum
    gain_dp[me] = exchange(gain_ctx, gc_send, gc_recv, "ctx", block, n_blocks)
    total = exchange(gain_dp, gd_send, gd_recv, "dp", me, n_ranks)
    q_sum_ref[...] = total[0:1, :]
    k_sum_ref[...] = total[1:2, :]

    def sent_dp(o):
        dest_copy(me, ahead(o), ahead(o)).wait_send()
        for c in range(CHUNKS):
            row_copy(c, ahead(o), me, ahead(o)).wait_send()
        gain_copy(gain_dp, gd_send, gd_recv, "dp", me, ahead(o)).wait_send()

    loop(n_ranks, sent_dp)
    loop(
        n_blocks,
        lambda o: gain_copy(
            gain_ctx, gc_send, gc_recv, "ctx", block, lax.rem(block + o, n_blocks)
        ).wait_send(),
    )
    for d in range(1, reach + 1):

        @pl.when(block + d < n_blocks)
        def _():
            docs_copy(d, block + d).wait_send()
            kv_copy(d, block + d).wait_send()

        @pl.when(block >= d)
        def _():
            for g in range(KEY_VALUE_HEADS):
                ret_copy(d, g, block - d).wait_send()


def per_device(n_ranks, n_blocks, rows, dest_rank, doc_ids, advantage, out_grad, q_gain, k_gain):
    tokens = rows.shape[1]
    width = rows.shape[2]
    reach = min(4, n_blocks - 1)
    capacity = tokens // n_ranks
    pitch = -(-capacity // 16) * 16
    slots = n_ranks * pitch
    keys = (reach + 1) * tokens
    stacked = GROUP * tokens
    vmem = pl.BlockSpec(memory_space=pltpu.VMEM)
    dma = pltpu.SemaphoreType.DMA
    attn, grads, q_sum, k_sum = pl.pallas_call(
        functools.partial(kernel, n_ranks, n_blocks, reach, capacity, pitch),
        out_shape=(
            jax.ShapeDtypeStruct((1, tokens, QUERY_WIDTH), bf16),
            jax.ShapeDtypeStruct((1, tokens, width), bf16),
            jax.ShapeDtypeStruct((1, HEAD_SIZE), f32),
            jax.ShapeDtypeStruct((1, HEAD_SIZE), f32),
        ),
        in_specs=[vmem] * 7,
        out_specs=(vmem,) * 4,
        scratch_shapes=[
            pltpu.VMEM((n_ranks, 1, tokens), jnp.int32),
            pltpu.VMEM((reach + 1, 1, tokens), jnp.int32),
            pltpu.VMEM((CHUNKS, slots, GROUP_WIDTH), bf16),
            pltpu.VMEM((CHUNKS, slots, GROUP_WIDTH), bf16),
            pltpu.VMEM((tokens, slots), bf16),
            pltpu.VMEM((tokens, GROUP_WIDTH), f32),
            pltpu.VMEM((KEY_VALUE_HEADS, keys, 2 * HEAD_SIZE), bf16),
            pltpu.VMEM((keys, 2 * tokens), f32),
            pltpu.VMEM((keys, stacked), bf16),
            pltpu.VMEM((keys, stacked), bf16),
            pltpu.VMEM((stacked, HEAD_SIZE), bf16),
            pltpu.VMEM((stacked, HEAD_SIZE), bf16),
            pltpu.VMEM((KEY_VALUE_HEADS, keys, 2 * HEAD_SIZE), bf16),
            pltpu.VMEM((reach, KEY_VALUE_HEADS, tokens, 2 * HEAD_SIZE), bf16),
            pltpu.VMEM((n_blocks, 8, HEAD_SIZE), f32),
            pltpu.VMEM((n_ranks, 8, HEAD_SIZE), f32),
            dma((n_ranks,)),
            dma((n_ranks,)),
            dma((reach,)),
            dma((reach,)),
            dma((CHUNKS, n_ranks)),
            dma((CHUNKS, n_ranks)),
            dma((reach,)),
            dma((reach,)),
            dma((reach, KEY_VALUE_HEADS)),
            dma((reach, KEY_VALUE_HEADS)),
            dma((n_blocks,)),
            dma((n_blocks,)),
            dma((n_ranks,)),
            dma((n_ranks,)),
        ],
        compiler_params=pltpu.CompilerParams(
            collective_id=0, has_side_effects=True, vmem_limit_bytes=48 * 1024 * 1024
        ),
        name="grpo_window",
    )(
        rows,
        dest_rank,
        doc_ids,
        advantage,
        out_grad,
        q_gain.reshape(1, HEAD_SIZE),
        k_gain.reshape(1, HEAD_SIZE),
    )
    return attn, grads, q_sum.reshape(HEAD_SIZE), k_sum.reshape(HEAD_SIZE)


def solution(mesh):
    placed = (
        P("dp", "ctx", None),
        P("dp", "ctx"),
        P("dp", "ctx"),
        P("dp", None),
        P("dp", "ctx", None),
        P(),
        P(),
    )
    return jax.shard_map(
        functools.partial(per_device, mesh.shape["dp"], mesh.shape["ctx"]),
        mesh=mesh,
        in_specs=placed,
        out_specs=(P("dp", "ctx", None), P("dp", "ctx", None), P(), P()),
        check_vma=False,
    )
```

time: 248 us -> 62.7 us (0.25)
  local copies, waits for them, and re-layouts: 61.7 us -> 8.86 us
  Pallas kernels: 0 us -> 52.3 us
  matrix products: 39.3 us -> 0 us
  starting transfers between devices: 38.1 us -> 0 us
  blocking collectives: 37 us -> 0 us
  other arithmetic: 35.1 us -> 0 us
  waiting for transfers between devices: 32.4 us -> 0 us
    pallas_call x0 -> x1, Pallas kernels: none -> 52.3 us  [per_device(): pl.pallas_call(functools.partial(kernel, n_ranks, n_blocks, reach, capaci...]
    dot_general x28 -> x0, matrix products: 39.3 us -> none  [the longest x4 6.66 us: head_backward(): jnp.einsum('tgd,sd->gts', q_part, k_part, preferred_element_type=jnp.floa...]
    psum x1 -> x0, blocking collectives: 37 us -> none  [per_device(): lax.psum((q_gain_part, k_gain_part), ('dp', 'ctx'))]
    ppermute x15 -> x0, starting transfers between devices: 28 us -> none  [passed_along(): return lax.ppermute(block, axis, route)]
    all_to_all x2 -> x0, waiting for transfers between devices: 27.5 us -> none  [the longest x1 24.3 us: per_device(): lax.all_to_all(outgoing, 'dp', split_axis=0, concat_axis=0, tiled=True)]
    scatter x2 -> x0, local copies, waits for them, and re-layouts: 23.6 us -> none  [the longest x1 19.8 us: per_device(): slot_table = jnp.full((n_ranks, capacity), -1, jnp.int32).at[peer_index,...]
    reduce_sum x8 -> x0, other arithmetic: 12.6 us -> none  [the longest x3 7.17 us: rms_scale(): values * lax.rsqrt(jnp.mean(values * values, axis=-1, keepdims=True) + ep...]
    all_to_all x2 -> x0, starting transfers between devices: 10.1 us -> none  [the longest x1 5.81 us: per_device(): lax.all_to_all(slot_table, 'dp', split_axis=0, concat_axis=0, tiled=True)]
  transfers between devices with their start and end apart: 17 -> 0, of which waited for: 4 -> 0; matrix products, arithmetic and copies ran while one was open for 29% -> 0% of each run, Pallas kernels for 0% -> 0%
where the time goes in v1:
time: 62.7 us; the launch traced here: 61.8 us
  Pallas kernels  52.3 us (83%)
  local copies, waits for them, and re-layouts  8.86 us (14%)
  between operations  0.66 us (1%)
    pallas_call x1, Pallas kernels, per_device(): pl.pallas_call(functools.partial(kernel, n_ranks, n_blocks, reach, capaci...  52.3 us
    unnamed x18, local copies, waits for them, and re-layouts  8.86 us

profile of v1, /device:TPU:0, one launch (start us, length us, event | category | flops | bytes accessed | tf_op | source)
XLA Modules:
  0.0 61.8 jit_solution(6335543480136420308)
XLA Ops:
  0.6 0.0 copy-start
  0.6 1.3 %copy-done = bf16[1,128,5120]{2,1,0:T(8,128)(2,1)S(1)} copy-done((bf16[1,128,5120]{2,1,0:T(8,128)(2,1)S(1)}, bf16[1,128,5120]{2,1,0:T(8,128)(2,1)}, u32[]{:S(2)}) %copy-start) | copy-done | bytes 1310744
  2.0 0.0 copy-start.1
  2.0 1.2 %copy-done.1 = bf16[1,128,4096]{2,1,0:T(8,128)(2,1)S(1)} copy-done((bf16[1,128,4096]{2,1,0:T(8,128)(2,1)S(1)}, bf16[1,128,4096]{2,1,0:T(8,128)(2,1)}, u32[]{:S(2)}) %copy-start.1) | copy-done | bytes 1048600
  3.2 0.0 copy-start.2
  3.2 0.7 %copy-done.2 = s32[1,128]{1,0:T(1,128)S(1)} copy-done((s32[1,128]{1,0:T(1,128)S(1)}, s32[1,128]{1,0:T(1,128)}, u32[]{:S(2)}) %copy-start.2) | copy-done | bytes 536
  3.8 0.0 copy-start.3
  3.8 0.7 %copy-done.3 = s32[1,128]{1,0:T(1,128)S(1)} copy-done((s32[1,128]{1,0:T(1,128)S(1)}, s32[1,128]{1,0:T(1,128)}, u32[]{:S(2)}) %copy-start.3) | copy-done | bytes 536
  4.5 0.0 copy-start.4
  4.5 0.7 %copy-done.4 = f32[1,6]{1,0:T(1,128)S(1)} copy-done((f32[1,6]{1,0:T(1,128)S(1)}, f32[1,6]{1,0:T(1,128)}, u32[]{:S(2)}) %copy-start.4) | copy-done | bytes 48
  5.1 0.0 copy-start.5
  5.1 0.7 %copy-done.5 = f32[128]{0:T(128)S(1)} copy-done((f32[128]{0:T(128)S(1)}, f32[128]{0:T(128)}, u32[]{:S(2)}) %copy-start.5) | copy-done | bytes 536
  5.8 0.0 copy-start.6
  5.8 0.7 %copy-done.6 = f32[128]{0:T(128)S(1)} copy-done((f32[128]{0:T(128)S(1)}, f32[128]{0:T(128)}, u32[]{:S(2)}) %copy-start.6) | copy-done | bytes 536
  6.5 52.3 %grpo_window.1 = (bf16[1,128,4096]{2,1,0:T(8,128)(2,1)S(1)}, bf16[1,128,5120]{2,1,0:T(8,128)(2,1)S(1)}, f32[1,128]{1,0:T(1,128)S(1)}, f32[1,128]{1,0:T(1,128)S(1)}) custom-call(bf16[1,128,5120]{2,1,0:T(8,128)(2,1)S(1)} %copy-done, s32[1,128]{1,0:T(1,128)S(1)} %copy-done.2, s32[1,128]{1,0:T(1,128)S(1)} %copy-done.3, f32[1,6]{1,0:T(1,128)S(1)} %copy-done.4, ...), custom_call_target="tpu_custom_call" | custom-call | tf_op jit(solution)/shard_map/grpo_window/pallas_call | solution.py:392
  58.8 1.0 %copy.15 = bf16[1,128,4096]{2,1,0:T(8,128)(2,1)} copy(bf16[1,128,4096]{2,1,0:T(8,128)(2,1)S(1)} %get-tuple-element.16) | data formatting | bytes 2097152
  59.8 1.1 %copy.16 = bf16[1,128,5120]{2,1,0:T(8,128)(2,1)} copy(bf16[1,128,5120]{2,1,0:T(8,128)(2,1)S(1)} %get-tuple-element.17) | data formatting | bytes 2621440
  60.8 0.5 copy.17
  61.3 0.5 copy.18
Async XLA Ops:
  0.6 1.3 %copy-start = (bf16[1,128,5120]{2,1,0:T(8,128)(2,1)S(1)}, bf16[1,128,5120]{2,1,0:T(8,128)(2,1)}, u32[]{:S(2)}) copy-start(bf16[1,128,5120]{2,1,0:T(8,128)(2,1)} %rows_ref.1) | copy-start | bytes 3932164
  2.0 1.2 %copy-start.1 = (bf16[1,128,4096]{2,1,0:T(8,128)(2,1)S(1)}, bf16[1,128,4096]{2,1,0:T(8,128)(2,1)}, u32[]{:S(2)}) copy-start(bf16[1,128,4096]{2,1,0:T(8,128)(2,1)} %grad_ref.1) | copy-start | bytes 3145732
  3.2 0.7 %copy-start.2 = (s32[1,128]{1,0:T(1,128)S(1)}, s32[1,128]{1,0:T(1,128)}, u32[]{:S(2)}) copy-start(s32[1,128]{1,0:T(1,128)} %dest_ref.1) | copy-start | bytes 1540
  3.8 0.7 %copy-start.3 = (s32[1,128]{1,0:T(1,128)S(1)}, s32[1,128]{1,0:T(1,128)}, u32[]{:S(2)}) copy-start(s32[1,128]{1,0:T(1,128)} %docs_ref.1) | copy-start | bytes 1540
  4.5 0.7 %copy-start.4 = (f32[1,6]{1,0:T(1,128)S(1)}, f32[1,6]{1,0:T(1,128)}, u32[]{:S(2)}) copy-start(f32[1,6]{1,0:T(1,128)} %adv_ref.1) | copy-start | bytes 76
  5.1 0.7 %copy-start.5 = (f32[128]{0:T(128)S(1)}, f32[128]{0:T(128)}, u32[]{:S(2)}) copy-start(f32[128]{0:T(128)} %param.12) | copy-start | bytes 1540
  5.8 0.7 %copy-start.6 = (f32[128]{0:T(128)S(1)}, f32[128]{0:T(128)}, u32[]{:S(2)}) copy-start(f32[128]{0:T(128)} %param.13) | copy-start | bytes 1540

commit v2 on v1

v2 whole, which is shorter than its diff:
```python
import functools
import math

import jax
import jax.numpy as jnp
from jax import lax
from jax.experimental import pallas as pl
from jax.experimental.pallas import tpu as pltpu
from jax.sharding import PartitionSpec as P

QUERY_HEADS = 32
KEY_VALUE_HEADS = 4
HEAD_SIZE = 128
GROUP = QUERY_HEADS // KEY_VALUE_HEADS
GROUP_WIDTH = GROUP * HEAD_SIZE
QUERY_WIDTH = QUERY_HEADS * HEAD_SIZE
KEY_WIDTH = KEY_VALUE_HEADS * HEAD_SIZE
HALF_WIDTH = GROUP_WIDTH // 2
CHUNKS = 2 * (KEY_VALUE_HEADS + 1)

epsilon = 1e-06
f32 = jnp.float32
bf16 = jnp.bfloat16
MESH = pl.DeviceIdType.MESH
LAST = (((1,), (1,)), ((), ()))


def matmul(a, b):
    return jnp.dot(a, b, preferred_element_type=f32)


def matmul_last(a, b):
    return lax.dot_general(a, b, LAST, preferred_element_type=f32)


def kernel(
    n_ranks, n_blocks, reach, capacity, pitch,
    rows_hbm, dest_hbm, docs_hbm, adv_hbm, grad_hbm, q_gain_hbm, k_gain_hbm,
    attn_hbm, out_hbm, gain_hbm,
    attn_ref, out_ref, gain_ref, out_sem, rows_ref, dest_ref, docs_ref, adv_ref, grad_ref, q_gain_ref, k_gain_ref, in_sem, rows_sem,
    dest_all, docs_all, send, recv, place, kv_win, allowed,
    prob_s, dscore_s, q_s, d_s, part, ret, gain_ctx, gain_dp, gain_all,
    dest_send, dest_recv, docs_send, docs_recv, row_send, row_recv,
    kv_send, kv_recv, ret_send, ret_recv, gc_send, gc_recv, gd_send, gd_recv, ga_send, ga_recv,
):
    tokens = rows_hbm.shape[1]
    me = lax.axis_index("dp")
    block = lax.axis_index("ctx")
    inverse = HEAD_SIZE ** (-0.5)

    barrier = pltpu.get_barrier_semaphore()

    def loop(stop, body):
        if stop <= 8:
            for o in range(stop - 1, 0, -1):
                body(o)
        else:
            lax.fori_loop(1, stop, lambda o, _: (body(stop - o), 0)[1], 0)

    def ahead(o):
        if n_ranks & (n_ranks - 1):
            return lax.rem(me + o, n_ranks)
        bit, other = 1, 0
        while bit < n_ranks:
            other = other + lax.rem(lax.div(me, bit) + lax.div(o, bit), 2) * bit
            bit = 2 * bit
        return other

    if n_ranks <= 8:
        partners = [None] + [ahead(o) for o in range(1, n_ranks)]
        ahead = partners.__getitem__

    def beside(o):
        return lax.rem(block + o, n_blocks)

    def greet(axis, other):
        pl.semaphore_signal(barrier, inc=1, device_id={axis: other}, device_id_type=MESH)

    everyone = n_ranks * n_blocks <= 64
    others = [(p, q) for p in range(n_ranks) for q in range(n_blocks)][1:] if everyone else []

    def device(p, q):
        to_dp = me if p == 0 else ahead(p)
        to_ctx = block if q == 0 else beside(q)
        return to_dp * n_blocks + to_ctx, {"dp": to_dp, "ctx": to_ctx}

    if everyone:
        for p, q in others:
            pl.semaphore_signal(
                barrier, inc=1, device_id=device(p, q)[1], device_id_type=MESH
            )
    else:
        loop(n_ranks, lambda o: greet("dp", ahead(o)))
        loop(n_blocks, lambda o: greet("ctx", beside(o)))

    def first_column(c):
        return QUERY_WIDTH + c * HALF_WIDTH if c < 2 else (c - 2) * HALF_WIDTH

    small = [
        pltpu.make_async_copy(src, dst, in_sem.at[i])
        for i, (src, dst) in enumerate(
            [
                (dest_hbm, dest_ref),
                (docs_hbm, docs_ref),
                (adv_hbm, adv_ref),
                (q_gain_hbm, q_gain_ref),
                (k_gain_hbm, k_gain_ref),
                (grad_hbm, grad_ref),
            ]
        )
    ]
    wide = [
        pltpu.make_async_copy(
            rows_hbm.at[0, :, pl.ds(first_column(c), HALF_WIDTH)], rows_ref.at[c], rows_sem.at[c]
        )
        for c in range(CHUNKS)
    ]
    small[0].start()
    small[1].start()
    for copy in wide:
        copy.start()
    for copy in small[2:]:
        copy.start()
    small[0].wait()
    small[1].wait()
    dest_all[me] = dest_ref[...]
    docs_all[0] = docs_ref[...]

    slots = n_ranks * pitch
    slot_row = lax.broadcasted_iota(jnp.int32, (slots, tokens), 0)
    slot_rank = slot_row // pitch
    slot_place = (slot_row % pitch).astype(f32)
    earlier = (
        lax.broadcasted_iota(jnp.int32, (tokens, tokens), 0)
        <= lax.broadcasted_iota(jnp.int32, (tokens, tokens), 1)
    ).astype(f32).astype(bf16)
    diagonal = lax.broadcasted_iota(jnp.int32, (tokens, tokens), 0) == lax.broadcasted_iota(
        jnp.int32, (tokens, tokens), 1
    )

    def slot_table(hit):
        hits = jnp.where(hit, 1.0, 0.0)
        count = matmul(hits.astype(bf16), earlier)
        return jnp.where(count - 1.0 == slot_place, hits, 0.0)

    def column(row):
        return jnp.sum(jnp.where(diagonal, row.astype(f32), 0.0), axis=1, keepdims=True)

    going = slot_table((dest_ref[...] == slot_rank) & (slot_rank != me)).astype(bf16)

    pl.semaphore_wait(barrier, len(others) if everyone else n_ranks - 1 + n_blocks - 1)

    def dest_copy(src, dst, to):
        return pltpu.make_async_remote_copy(
            src_ref=dest_all.at[src],
            dst_ref=dest_all.at[src],
            send_sem=dest_send.at[dst],
            recv_sem=dest_recv.at[src],
            device_id={"dp": to},
            device_id_type=MESH,
        )

    def row_copy(c, slot, home, to):
        return pltpu.make_async_remote_copy(
            src_ref=send.at[c, pl.ds(pl.multiple_of(slot * pitch, 16), pitch), :],
            dst_ref=recv.at[c, pl.ds(pl.multiple_of(home * pitch, 16), pitch), :],
            send_sem=row_send.at[c, slot],
            recv_sem=row_recv.at[c, home],
            device_id={"dp": to},
            device_id_type=MESH,
        )

    def docs_copy(d, to):
        return pltpu.make_async_remote_copy(
            src_ref=docs_all.at[0],
            dst_ref=docs_all.at[d],
            send_sem=docs_send.at[d - 1],
            recv_sem=docs_recv.at[d - 1],
            device_id={"ctx": to},
            device_id_type=MESH,
        )

    def kv_copy(d, to):
        return pltpu.make_async_remote_copy(
            src_ref=kv_win.at[:, pl.ds(0, tokens), :],
            dst_ref=kv_win.at[:, pl.ds(d * tokens, tokens), :],
            send_sem=kv_send.at[d - 1],
            recv_sem=kv_recv.at[d - 1],
            device_id={"ctx": to},
            device_id_type=MESH,
        )

    def ret_copy(d, g, to):
        return pltpu.make_async_remote_copy(
            src_ref=part.at[g, pl.ds(d * tokens, tokens), :],
            dst_ref=ret.at[d - 1, g],
            send_sem=ret_send.at[d - 1, g],
            recv_sem=ret_recv.at[d - 1, g],
            device_id={"ctx": to},
            device_id_type=MESH,
        )

    loop(n_ranks, lambda o: dest_copy(me, ahead(o), ahead(o)).start())
    for d in range(1, reach + 1):

        @pl.when(block + d < n_blocks)
        def _():
            docs_copy(d, block + d).start()

    for c in range(CHUNKS):
        wide[c].wait()
        send[c] = matmul(going, rows_ref[c]).astype(bf16)
        loop(n_ranks, lambda o: row_copy(c, ahead(o), me, ahead(o)).start())

    for copy in small[2:]:
        copy.wait()
    gain_ctx[block] = jnp.zeros((8, HEAD_SIZE), f32)
    gain_ref[...] = jnp.zeros((8, HEAD_SIZE), f32)
    for c in range(CHUNKS):
        recv[c, pl.ds(pl.multiple_of(me * pitch, 16), pitch), :] = jnp.zeros(
            (pitch, HALF_WIDTH), bf16
        )
    for d in range(1, reach + 1):

        @pl.when(block < d)
        def _():
            docs_all[d] = jnp.full((1, tokens), -1, jnp.int32)
            kv_win[:, d * tokens : (d + 1) * tokens, :] = jnp.zeros(
                (KEY_VALUE_HEADS, tokens, 2 * HEAD_SIZE), bf16
            )

        @pl.when(block + d >= n_blocks)
        def _():
            ret[d - 1] = jnp.zeros((KEY_VALUE_HEADS, tokens, 2 * HEAD_SIZE), bf16)

    loop(n_ranks, lambda o: dest_copy(ahead(o), me, ahead(o)).wait_recv())
    source = jnp.broadcast_to(dest_all[...], (n_ranks, pitch, tokens)).reshape(slots, tokens)
    coming = slot_table((source == me) & (slot_rank != me))
    place[...] = jnp.transpose(coming).astype(bf16)
    staying = column(jnp.where(dest_ref[...] == me, 1.0, 0.0))
    doc_column = column(docs_ref[...])
    advantage = jnp.zeros((tokens, 1), f32)
    for doc in range(adv_ref.shape[1]):
        advantage = advantage + jnp.where(
            doc_column == float(doc), adv_ref[0:1, doc : doc + 1], 0.0
        )

    def packed(c):
        loop(n_ranks, lambda o: row_copy(c, me, ahead(o), ahead(o)).wait_recv())
        return matmul(place[...], recv[c]) + rows_ref[c].astype(f32) * staying

    def unit(values):
        scale = lax.rsqrt(jnp.mean(values * values, axis=-1, keepdims=True) + epsilon)
        return values * scale, scale

    for half in range(2):
        raw = packed(half).astype(bf16)
        for g in range(KEY_VALUE_HEADS):
            kv_win[g, 0:tokens, half * HEAD_SIZE : (half + 1) * HEAD_SIZE] = raw[
                :, g * HEAD_SIZE : (g + 1) * HEAD_SIZE
            ]
    for d in range(1, reach + 1):

        @pl.when(block + d < n_blocks)
        def _():
            kv_copy(d, block + d).start()

    for d in range(1, reach + 1):

        @pl.when(block >= d)
        def _():
            docs_copy(d, block - d).wait_recv()

    my_docs = docs_ref[...].astype(f32)
    for d in range(reach + 1):
        same = column(docs_all[d]) == my_docs
        if d == 0:
            same = same & (
                lax.broadcasted_iota(jnp.int32, (tokens, tokens), 0)
                <= lax.broadcasted_iota(jnp.int32, (tokens, tokens), 1)
            )
        same = jnp.where(same, 1.0, 0.0)
        allowed[d * tokens : (d + 1) * tokens, 0:tokens] = same
        allowed[d * tokens : (d + 1) * tokens, tokens : 2 * tokens] = same

    for d in range(1, reach + 1):

        @pl.when(block >= d)
        def _():
            kv_copy(d, block - d).wait_recv()

    def group_columns(g):
        return pl.ds(pl.multiple_of(g * GROUP_WIDTH, GROUP_WIDTH), GROUP_WIDTH)

    def attn_out_copy(g):
        return pltpu.make_async_copy(
            attn_ref.at[:, :, group_columns(g)], attn_hbm.at[:, :, group_columns(g)], out_sem.at[0, g]
        )

    def query_out_copy(g):
        return pltpu.make_async_copy(
            out_ref.at[:, :, group_columns(g)], out_hbm.at[:, :, group_columns(g)], out_sem.at[1, g]
        )

    def give_back(g):
        for d in range(1, reach + 1):

            @pl.when(block >= d)
            def _():
                ret_copy(d, g, block - d).start()

    def one_group(g, sums):
        q_gain_sum, k_gain_sum = sums
        first = pl.multiple_of(g * GROUP_WIDTH, GROUP_WIDTH)
        k_unit, _ = unit(kv_win[g, :, 0:HEAD_SIZE].astype(f32))
        k = (k_unit * k_gain_ref[...]).astype(bf16)
        v = kv_win[g, :, HEAD_SIZE : 2 * HEAD_SIZE]
        k_across = jnp.transpose(k.astype(f32)).astype(bf16)
        v_across = jnp.transpose(v.astype(f32)).astype(bf16)
        for pair in range(GROUP // 2):
            if pair % (GROUP // 4) == 0:
                half = pair // (GROUP // 4)
                raw = packed(2 * g + 2 + half)
                base = pl.multiple_of(first + half * HALF_WIDTH, HALF_WIDTH)
                grads = (
                    grad_ref[0, :, pl.ds(base, HALF_WIDTH)].astype(f32) * advantage
                ).astype(bf16)
            at = pair % (GROUP // 4)
            a = slice(2 * at * HEAD_SIZE, (2 * at + 1) * HEAD_SIZE)
            b = slice((2 * at + 1) * HEAD_SIZE, (2 * at + 2) * HEAD_SIZE)
            across = slice(pair * 2 * tokens, (pair + 1) * 2 * tokens)
            q_unit, q_scale = unit(jnp.concatenate([raw[:, a], raw[:, b]], axis=0))
            q_hat = (q_unit * q_gain_ref[...]).astype(bf16)
            d_out = jnp.concatenate([grads[:, a], grads[:, b]], axis=0)
            score = matmul_last(k, q_hat)
            weight = jnp.exp2(score * (inverse * math.log2(math.e))) * allowed[...]
            total = jnp.sum(weight, axis=0, keepdims=True)
            share = 1.0 / total
            attn = (matmul(v_across, weight.astype(bf16)) * share).astype(bf16).astype(f32)
            delta = jnp.sum(jnp.transpose(d_out.astype(f32)) * attn, axis=0, keepdims=True)
            attn_rows = jnp.transpose(attn).astype(bf16)
            prob = weight * share
            dscore = (prob * (matmul_last(v, d_out) - delta)).astype(bf16)
            prob_s[:, across] = prob.astype(bf16)
            dscore_s[:, across] = dscore
            q_s[across, :] = q_hat
            d_s[across, :] = d_out
            dq_hat = jnp.transpose(matmul(k_across, dscore)) * inverse
            q_gain_sum = q_gain_sum + jnp.sum(dq_hat * q_unit, axis=0, keepdims=True)
            scaled = dq_hat * q_gain_ref[...]
            dq = (
                q_scale * (scaled - q_unit * jnp.mean(scaled * q_unit, axis=-1, keepdims=True))
            ).astype(bf16)
            for i, where in ((0, a), (1, b)):
                cols = pl.ds(pl.multiple_of(base + where.start, HEAD_SIZE), HEAD_SIZE)
                attn_ref[0, :, cols] = attn_rows[i * tokens : (i + 1) * tokens]
                out_ref[0, :, cols] = dq[i * tokens : (i + 1) * tokens]
        dk_part = (matmul(dscore_s[...], q_s[...]) * inverse).astype(bf16)
        part[g, :, 0:HEAD_SIZE] = dk_part
        part[g, :, HEAD_SIZE : 2 * HEAD_SIZE] = matmul(prob_s[...], d_s[...]).astype(bf16)
        @pl.when(g < KEY_VALUE_HEADS - 1)
        def _():
            give_back(g)

        attn_out_copy(g).start()
        query_out_copy(g).start()

        k_gain_sum = k_gain_sum + jnp.sum(dk_part.astype(f32) * k_unit, axis=0, keepdims=True)
        return q_gain_sum, k_gain_sum

    none = jnp.zeros((1, HEAD_SIZE), f32)
    q_gain_sum, k_gain_sum = lax.fori_loop(0, KEY_VALUE_HEADS, one_group, (none, none))

    def gain_copy(buffer, send_sems, recv_sems, axis, home, to, other):
        return pltpu.make_async_remote_copy(
            src_ref=buffer.at[home],
            dst_ref=buffer.at[to],
            send_sem=send_sems.at[other],
            recv_sem=recv_sems.at[to],
            device_id={axis: other},
            device_id_type=MESH,
        )

    over_ctx = functools.partial(gain_copy, gain_ctx, gc_send, gc_recv, "ctx", block)
    over_dp = functools.partial(gain_copy, gain_dp, gd_send, gd_recv, "dp", me)

    def summed(buffer, count):
        total = buffer[0]
        for i in range(1, count):
            total = total + buffer[i]
        return total

    def gain_to(p, q):
        home = me * n_blocks + block
        index, to = device(p, q)
        return pltpu.make_async_remote_copy(
            src_ref=gain_all.at[home],
            dst_ref=gain_all.at[home],
            send_sem=ga_send.at[index],
            recv_sem=ga_recv.at[home],
            device_id=to,
            device_id_type=MESH,
        )

    def gain_from(p, q):
        index, to = device(p, q)
        return pltpu.make_async_remote_copy(
            src_ref=gain_all.at[index],
            dst_ref=gain_all.at[index],
            send_sem=ga_send.at[index],
            recv_sem=ga_recv.at[index],
            device_id=to,
            device_id_type=MESH,
        )

    if everyone:
        gain_all[me * n_blocks + block, 0:1, :] = q_gain_sum
        gain_all[me * n_blocks + block, 1:2, :] = k_gain_sum
        for p, q in others:
            gain_to(p, q).start()
        give_back(KEY_VALUE_HEADS - 1)
    else:
        give_back(KEY_VALUE_HEADS - 1)
        gain_ctx[block, 0:1, :] = q_gain_sum
        gain_ctx[block, 1:2, :] = k_gain_sum
        loop(n_blocks, lambda o: over_ctx(block, beside(o)).start())
        loop(n_blocks, lambda o: over_ctx(beside(o), beside(o)).wait_recv())
        gain_dp[me] = summed(gain_ctx, n_blocks)
        loop(n_ranks, lambda o: over_dp(me, ahead(o)).start())

    for d in range(1, reach + 1):

        @pl.when(block + d < n_blocks)
        def _():
            for g in range(KEY_VALUE_HEADS):
                ret_copy(d, g, block + d).wait_recv()

    for g in range(KEY_VALUE_HEADS):
        both = part[g, 0:tokens, :].astype(f32)
        for d in range(1, reach + 1):
            both = both + ret[d - 1, g].astype(f32)
        k_unit, k_scale = unit(kv_win[g, 0:tokens, 0:HEAD_SIZE].astype(f32))
        scaled = both[:, 0:HEAD_SIZE] * k_gain_ref[...]
        dk = k_scale * (scaled - k_unit * jnp.mean(scaled * k_unit, axis=-1, keepdims=True))
        at = QUERY_WIDTH + g * HEAD_SIZE
        out_ref[0, :, at : at + HEAD_SIZE] = dk.astype(bf16)
        at = at + KEY_WIDTH
        out_ref[0, :, at : at + HEAD_SIZE] = both[:, HEAD_SIZE:].astype(bf16)

    last = pl.ds(QUERY_WIDTH, 2 * KEY_WIDTH)
    last_out = pltpu.make_async_copy(
        out_ref.at[:, :, last], out_hbm.at[:, :, last], out_sem.at[0, KEY_VALUE_HEADS]
    )
    last_out.start()
    if everyone:
        for p, q in others:
            gain_from(p, q).wait_recv()
        gain_ref[0:2, :] = jnp.sum(gain_all[...], axis=0)
    else:
        loop(n_ranks, lambda o: over_dp(ahead(o), ahead(o)).wait_recv())
        gain_ref[...] = summed(gain_dp, n_ranks)
    gain_out = pltpu.make_async_copy(gain_ref, gain_hbm, out_sem.at[1, KEY_VALUE_HEADS])
    gain_out.start()

    for g in range(KEY_VALUE_HEADS):
        attn_out_copy(g).wait()
        query_out_copy(g).wait()
    last_out.wait()
    gain_out.wait()
    def sent_dp(o):
        dest_copy(me, ahead(o), ahead(o)).wait_send()
        for c in range(CHUNKS):
            row_copy(c, ahead(o), me, ahead(o)).wait_send()
        if not everyone:
            over_dp(me, ahead(o)).wait_send()

    loop(n_ranks, sent_dp)
    for p, q in others:
        gain_to(p, q).wait_send()
    if not everyone:
        loop(n_blocks, lambda o: over_ctx(block, beside(o)).wait_send())
    for d in range(1, reach + 1):

        @pl.when(block + d < n_blocks)
        def _():
            docs_copy(d, block + d).wait_send()
            kv_copy(d, block + d).wait_send()

        @pl.when(block >= d)
        def _():
            for g in range(KEY_VALUE_HEADS):
                ret_copy(d, g, block - d).wait_send()


def write_out(attn_in, grads_in, gains, attn, grads, q_sum, k_sum, attn_v, grads_v, gains_v, in_sems, out_sems):
    ways = [(gains, gains_v, gains_v.at[pl.ds(0, 1), :], q_sum)]
    step = attn_in.shape[1] // 4
    for i in range(4):
        rows = (slice(None), pl.ds(i * step, step), slice(None))
        ways.append((attn_in.at[rows], attn_v.at[rows], attn_v.at[rows], attn.at[rows]))
        ways.append((grads_in.at[rows], grads_v.at[rows], grads_v.at[rows], grads.at[rows]))
    come = [pltpu.make_async_copy(w[0], w[1], in_sems.at[i]) for i, w in enumerate(ways)]
    go = [pltpu.make_async_copy(w[2], w[3], out_sems.at[i]) for i, w in enumerate(ways)]
    second = pltpu.make_async_copy(gains_v.at[pl.ds(1, 1), :], k_sum, out_sems.at[len(ways)])
    for copy in come:
        copy.start()
    for i in range(len(ways)):
        come[i].wait()
        go[i].start()
        if i == 0:
            second.start()
    for copy in go:
        copy.wait()
    second.wait()


def per_device(n_ranks, n_blocks, rows, dest_rank, doc_ids, advantage, out_grad, q_gain, k_gain):
    tokens = rows.shape[1]
    width = rows.shape[2]
    reach = min(4, n_blocks - 1)
    capacity = tokens // n_ranks
    pitch = -(-capacity // 16) * 16
    slots = n_ranks * pitch
    keys = (reach + 1) * tokens
    stacked = GROUP * tokens
    direct = n_ranks * n_blocks if n_ranks * n_blocks <= 64 else 1
    dma = pltpu.SemaphoreType.DMA
    hbm = pl.BlockSpec(memory_space=pltpu.HBM)
    results = (
        jax.ShapeDtypeStruct((1, tokens, QUERY_WIDTH), bf16),
        jax.ShapeDtypeStruct((1, tokens, width), bf16),
        jax.ShapeDtypeStruct((1, HEAD_SIZE), f32),
        jax.ShapeDtypeStruct((1, HEAD_SIZE), f32),
    )
    partial = pl.pallas_call(
        functools.partial(kernel, n_ranks, n_blocks, reach, capacity, pitch),
        out_shape=(*results[:2], jax.ShapeDtypeStruct((8, HEAD_SIZE), f32)),
        in_specs=[hbm] * 7,
        out_specs=(hbm,) * 3,
        scratch_shapes=[
            pltpu.VMEM((1, tokens, QUERY_WIDTH), bf16),
            pltpu.VMEM((1, tokens, width), bf16),
            pltpu.VMEM((8, HEAD_SIZE), f32),
            dma((2, KEY_VALUE_HEADS + 1)),
            pltpu.VMEM((CHUNKS, tokens, HALF_WIDTH), bf16),
            pltpu.VMEM((1, tokens), jnp.int32),
            pltpu.VMEM((1, tokens), jnp.int32),
            pltpu.VMEM(advantage.shape, f32),
            pltpu.VMEM((1, tokens, QUERY_WIDTH), bf16),
            pltpu.VMEM((1, HEAD_SIZE), f32),
            pltpu.VMEM((1, HEAD_SIZE), f32),
            dma((6,)),
            dma((CHUNKS,)),
            pltpu.VMEM((n_ranks, 1, tokens), jnp.int32),
            pltpu.VMEM((reach + 1, 1, tokens), jnp.int32),
            pltpu.VMEM((CHUNKS, slots, HALF_WIDTH), bf16),
            pltpu.VMEM((CHUNKS, slots, HALF_WIDTH), bf16),
            pltpu.VMEM((tokens, slots), bf16),
            pltpu.VMEM((KEY_VALUE_HEADS, keys, 2 * HEAD_SIZE), bf16),
            pltpu.VMEM((keys, 2 * tokens), f32),
            pltpu.VMEM((keys, stacked), bf16),
            pltpu.VMEM((keys, stacked), bf16),
            pltpu.VMEM((stacked, HEAD_SIZE), bf16),
            pltpu.VMEM((stacked, HEAD_SIZE), bf16),
            pltpu.VMEM((KEY_VALUE_HEADS, keys, 2 * HEAD_SIZE), bf16),
            pltpu.VMEM((reach, KEY_VALUE_HEADS, tokens, 2 * HEAD_SIZE), bf16),
            pltpu.VMEM((n_blocks, 8, HEAD_SIZE), f32),
            pltpu.VMEM((n_ranks, 8, HEAD_SIZE), f32),
            pltpu.VMEM((direct, 2, HEAD_SIZE), f32),
            dma((n_ranks,)),
            dma((n_ranks,)),
            dma((reach,)),
            dma((reach,)),
            dma((CHUNKS, n_ranks)),
            dma((CHUNKS, n_ranks)),
            dma((reach,)),
            dma((reach,)),
            dma((reach, KEY_VALUE_HEADS)),
            dma((reach, KEY_VALUE_HEADS)),
            dma((n_blocks,)),
            dma((n_blocks,)),
            dma((n_ranks,)),
            dma((n_ranks,)),
            dma((direct,)),
            dma((direct,)),
        ],
        compiler_params=pltpu.CompilerParams(
            collective_id=0, has_side_effects=True, vmem_limit_bytes=62 * 1024 * 1024
        ),
        name="grpo_window",
    )(
        rows,
        dest_rank,
        doc_ids,
        advantage,
        out_grad,
        q_gain.reshape(1, HEAD_SIZE),
        k_gain.reshape(1, HEAD_SIZE),
    )
    attn, grads, q_sum, k_sum = pl.pallas_call(
        write_out,
        out_shape=results,
        in_specs=[hbm] * 3,
        out_specs=(hbm,) * 4,
        scratch_shapes=[
            pltpu.VMEM((1, tokens, QUERY_WIDTH), bf16),
            pltpu.VMEM((1, tokens, width), bf16),
            pltpu.VMEM(partial[2].shape, f32),
            dma((9,)),
            dma((10,)),
        ],
        compiler_params=pltpu.CompilerParams(vmem_limit_bytes=62 * 1024 * 1024),
        name="write_out",
    )(*partial)
    return attn, grads, q_sum.reshape(HEAD_SIZE), k_sum.reshape(HEAD_SIZE)


def solution(mesh):
    placed = (
        P("dp", "ctx", None),
        P("dp", "ctx"),
        P("dp", "ctx"),
        P("dp", None),
        P("dp", "ctx", None),
        P(),
        P(),
    )
    return jax.shard_map(
        functools.partial(per_device, mesh.shape["dp"], mesh.shape["ctx"]),
        mesh=mesh,
        in_specs=placed,
        out_specs=(P("dp", "ctx", None), P("dp", "ctx", None), P(), P()),
        check_vma=False,
    )
```

time: 62.7 us -> 58.7 us (0.936); the launches traced: 61.8 us -> 58.6 us
  local copies, waits for them, and re-layouts: 8.86 us -> 0 us
  Pallas kernels: 52.3 us -> 57.9 us
    unnamed x18 -> x0, local copies, waits for them, and re-layouts: 8.86 us -> none
    pallas_call x1, Pallas kernels: 52.3 us -> 55.4 us  [per_device(): pl.pallas_call(functools.partial(kernel, n_ranks, n_blocks, reach, capaci...]
    pallas_call x0 -> x1, Pallas kernels: none -> 2.53 us  [per_device(): pl.pallas_call(write_out, out_shape=results, in_specs=[hbm] * 3, out_spec...]
where the time goes in v2:
time: 58.7 us; the launch traced here: 58.6 us
  Pallas kernels  57.9 us (99%)
  between operations  0.64 us (1%)
    pallas_call x1, Pallas kernels, per_device(): pl.pallas_call(functools.partial(kernel, n_ranks, n_blocks, reach, capaci...  55.4 us
    pallas_call x1, Pallas kernels, per_device(): pl.pallas_call(write_out, out_shape=results, in_specs=[hbm] * 3, out_spec...  2.53 us

profile of v2, /device:TPU:0, one launch (start us, length us, event | category | flops | bytes accessed | tf_op | source)
XLA Modules:
  0.0 58.6 jit_solution(2281535317565353783)
XLA Ops:
  0.6 55.4 %grpo_window.1 = (bf16[1,128,4096]{2,1,0:T(8,128)(2,1)}, bf16[1,128,5120]{2,1,0:T(8,128)(2,1)}, f32[8,128]{1,0:T(8,128)}) custom-call(bf16[1,128,5120]{2,1,0:T(8,128)(2,1)} %rows_hbm.1, s32[1,128]{1,0:T(1,128)} %dest_hbm.1, s32[1,128]{1,0:T(1,128)} %docs_hbm.1, f32[1,6]{1,0:T(1,128)} %adv_hbm.1, bf16[1,128,4096]{2,1,0:T(8,128)(2,1)} %grad_hbm.1, ...), custom_call_target="tpu_custom_call" | custom-call | tf_op jit(solution)/shard_map/grpo_window/pallas_call | solution.py:535
  56.0 2.5 %write_out.1 = (bf16[1,128,4096]{2,1,0:T(8,128)(2,1)}, bf16[1,128,5120]{2,1,0:T(8,128)(2,1)}, f32[1,128]{1,0:T(1,128)}, f32[1,128]{1,0:T(1,128)}) custom-call(bf16[1,128,4096]{2,1,0:T(8,128)(2,1)} %get-tuple-element.11.attn_in, bf16[1,128,5120]{2,1,0:T(8,128)(2,1)} %get-tuple-element.12.grads_in, f32[8,128]{1,0:T(8,128)} %get-tuple-element.13.gains), custom_call_target="tpu_custom_call" | custom-call | tf_op jit(solution)/shard_map/write_out/pallas_call | solution.py:600

commit v3 on v2

--- a/solution.py
+++ b/solution.py
@@ -52,7 +52,7 @@
 
     def loop(stop, body):
         if stop <= 8:
-            for o in range(stop - 1, 0, -1):
+            for o in range(1, stop):
                 body(o)
         else:
             lax.fori_loop(1, stop, lambda o, _: (body(stop - o), 0)[1], 0)
@@ -75,23 +75,6 @@
 
     def greet(axis, other):
         pl.semaphore_signal(barrier, inc=1, device_id={axis: other}, device_id_type=MESH)
-
-    everyone = n_ranks * n_blocks <= 64
-    others = [(p, q) for p in range(n_ranks) for q in range(n_blocks)][1:] if everyone else []
-
-    def device(p, q):
-        to_dp = me if p == 0 else ahead(p)
-        to_ctx = block if q == 0 else beside(q)
-        return to_dp * n_blocks + to_ctx, {"dp": to_dp, "ctx": to_ctx}
-
-    if everyone:
-        for p, q in others:
-            pl.semaphore_signal(
-                barrier, inc=1, device_id=device(p, q)[1], device_id_type=MESH
-            )
-    else:
-        loop(n_ranks, lambda o: greet("dp", ahead(o)))
-        loop(n_blocks, lambda o: greet("ctx", beside(o)))
 
     def first_column(c):
         return QUERY_WIDTH + c * HALF_WIDTH if c < 2 else (c - 2) * HALF_WIDTH
@@ -116,8 +99,27 @@
         for c in range(CHUNKS)
     ]
     small[0].start()
+    wide[0].start()
+
+    everyone = n_ranks * n_blocks <= 64
+    others = [(p, q) for p in range(n_ranks) for q in range(n_blocks)][1:] if everyone else []
+
+    def device(p, q):
+        to_dp = me if p == 0 else ahead(p)
+        to_ctx = block if q == 0 else beside(q)
+        return to_dp * n_blocks + to_ctx, {"dp": to_dp, "ctx": to_ctx}
+
+    if everyone:
+        for p, q in others:
+            pl.semaphore_signal(
+                barrier, inc=1, device_id=device(p, q)[1], device_id_type=MESH
+            )
+    else:
+        loop(n_ranks, lambda o: greet("dp", ahead(o)))
+        loop(n_blocks, lambda o: greet("ctx", beside(o)))
+
     small[1].start()
-    for copy in wide:
+    for copy in wide[1:]:
         copy.start()
     for copy in small[2:]:
         copy.start()
@@ -428,14 +430,35 @@
         gain_dp[me] = summed(gain_ctx, n_blocks)
         loop(n_ranks, lambda o: over_dp(me, ahead(o)).start())
 
+    def sent_dp(o):
+        dest_copy(me, ahead(o), ahead(o)).wait_send()
+        for c in range(CHUNKS):
+            row_copy(c, ahead(o), me, ahead(o)).wait_send()
+
+    loop(n_ranks, sent_dp)
     for d in range(1, reach + 1):
 
         @pl.when(block + d < n_blocks)
         def _():
-            for g in range(KEY_VALUE_HEADS):
+            docs_copy(d, block + d).wait_send()
+            kv_copy(d, block + d).wait_send()
+
+        @pl.when(block >= d)
+        def _():
+            for g in range(KEY_VALUE_HEADS - 1):
+                ret_copy(d, g, block - d).wait_send()
+
+    for g in range(KEY_VALUE_HEADS):
+        attn_out_copy(g).wait()
+        query_out_copy(g).wait()
+
+    for g in range(KEY_VALUE_HEADS):
+        for d in range(1, reach + 1):
+
+            @pl.when(block + d < n_blocks)
+            def _():
                 ret_copy(d, g, block + d).wait_recv()
 
-    for g in range(KEY_VALUE_HEADS):
         both = part[g, 0:tokens, :].astype(f32)
         for d in range(1, reach + 1):
             both = both + ret[d - 1, g].astype(f32)
@@ -462,34 +485,19 @@
     gain_out = pltpu.make_async_copy(gain_ref, gain_hbm, out_sem.at[1, KEY_VALUE_HEADS])
     gain_out.start()
 
-    for g in range(KEY_VALUE_HEADS):
-        attn_out_copy(g).wait()
-        query_out_copy(g).wait()
-    last_out.wait()
-    gain_out.wait()
-    def sent_dp(o):
-        dest_copy(me, ahead(o), ahead(o)).wait_send()
-        for c in range(CHUNKS):
-            row_copy(c, ahead(o), me, ahead(o)).wait_send()
-        if not everyone:
-            over_dp(me, ahead(o)).wait_send()
-
-    loop(n_ranks, sent_dp)
     for p, q in others:
         gain_to(p, q).wait_send()
     if not everyone:
+        loop(n_ranks, lambda o: over_dp(me, ahead(o)).wait_send())
         loop(n_blocks, lambda o: over_ctx(block, beside(o)).wait_send())
     for d in range(1, reach + 1):
 
-        @pl.when(block + d < n_blocks)
-        def _():
-            docs_copy(d, block + d).wait_send()
-            kv_copy(d, block + d).wait_send()
-
         @pl.when(block >= d)
         def _():
-            for g in range(KEY_VALUE_HEADS):
-                ret_copy(d, g, block - d).wait_send()
+            ret_copy(d, KEY_VALUE_HEADS - 1, block - d).wait_send()
+
+    last_out.wait()
+    gain_out.wait()
 
 
 def write_out(attn_in, grads_in, gains, attn, grads, q_sum, k_sum, attn_v, grads_v, gains_v, in_sems, out_sems):

time: 58.7 us -> 55.8 us (0.951)
  Pallas kernels: 57.9 us -> 54.9 us
    pallas_call x1, Pallas kernels: 55.4 us -> 52.4 us  [per_device(): pl.pallas_call(functools.partial(kernel, n_ranks, n_blocks, reach, capaci...]
where the time goes in v3:
time: 55.8 us; the launch traced here: 55.6 us
  Pallas kernels  54.9 us (98%)
  between operations  0.64 us (1%)
    pallas_call x1, Pallas kernels, per_device(): pl.pallas_call(functools.partial(kernel, n_ranks, n_blocks, reach, capaci...  52.4 us
    pallas_call x1, Pallas kernels, per_device(): pl.pallas_call(write_out, out_shape=results, in_specs=[hbm] * 3, out_spec...  2.53 us

profile of v3, /device:TPU:0, one launch (start us, length us, event | category | flops | bytes accessed | tf_op | source)
XLA Modules:
  0.0 55.6 jit_solution(2419578095493490839)
XLA Ops:
  0.6 52.4 %grpo_window.1 = (bf16[1,128,4096]{2,1,0:T(8,128)(2,1)}, bf16[1,128,5120]{2,1,0:T(8,128)(2,1)}, f32[8,128]{1,0:T(8,128)}) custom-call(bf16[1,128,5120]{2,1,0:T(8,128)(2,1)} %rows_hbm.1, s32[1,128]{1,0:T(1,128)} %dest_hbm.1, s32[1,128]{1,0:T(1,128)} %docs_hbm.1, f32[1,6]{1,0:T(1,128)} %adv_hbm.1, bf16[1,128,4096]{2,1,0:T(8,128)(2,1)} %grad_hbm.1, ...), custom_call_target="tpu_custom_call" | custom-call | tf_op jit(solution)/shard_map/grpo_window/pallas_call | solution.py:543
  53.0 2.5 %write_out.1 = (bf16[1,128,4096]{2,1,0:T(8,128)(2,1)}, bf16[1,128,5120]{2,1,0:T(8,128)(2,1)}, f32[1,128]{1,0:T(1,128)}, f32[1,128]{1,0:T(1,128)}) custom-call(bf16[1,128,4096]{2,1,0:T(8,128)(2,1)} %get-tuple-element.11.attn_in, bf16[1,128,5120]{2,1,0:T(8,128)(2,1)} %get-tuple-element.12.grads_in, f32[8,128]{1,0:T(8,128)} %get-tuple-element.13.gains), custom_call_target="tpu_custom_call" | custom-call | tf_op jit(solution)/shard_map/write_out/pallas_call | solution.py:608
